TPU v7x, 256 devices: a whole 4x4x8 slice. The times are simulated.
256 devices in a mesh: frame: 16 (over z_hi, x, core), within: 16 (over y, z_lo).
Axes of the slice: x: 4, y: 4, z: 8 (z_hi: 2, z_lo: 4; z = z_hi * 4 + z_lo), core: 2. Of those that a mesh axis runs over, the one named last changes fastest.
Arguments:
- queries: bfloat16 [16, 1152, 1024], P('frame', 'within'), may hold values from -6 to 6
- keys_in: bfloat16 [16, 1152, 1024], P('frame', 'within'), may hold values from -6 to 6
- values_in: bfloat16 [16, 1152, 1024], P('frame', 'within'), may hold values from -6 to 6
- grad_out: bfloat16 [16, 1152, 1024], P('frame', 'within'), may hold values from -6 to 6
- partners: int32 [16, 2], replicated, may hold values from 0 to 15
- registers: int32 [16], replicated, may hold values from 1 to 288
Outputs:
- grad_queries: bfloat16 [16, 1152, 1024], P('frame', 'within')
- grad_keys: bfloat16 [16, 1152, 1024], P('frame', 'within')
- grad_values: bfloat16 [16, 1152, 1024], P('frame', 'within')
Inputs may be any that keep to these rules, and one draw needn't show every extreme that they name: `partners`: A row may list a group more than once, and may list its own group.
All inputs are finite; a program needn't handle non-finite values.
Results may differ from a plain program's by a relative error of at most 0.012.
Values may be sent and summed in bfloat16 or wider, within the bound.
No kernel may reach another device: no remote copies, remote signals or barrier semaphores. Data moves between devices by JAX's collectives and lax.ppermute only.
A program may use at most 128 MiB of HBM per device.

v0:
```python
import jax
import jax.numpy as jnp
from jax import lax
from jax.sharding import PartitionSpec as P

DH = 64


def local(queries, keys_in, values_in, grad_out, partners, registers):
    q_wide, k_wide, v_wide, d_wide = (
        lax.all_to_all(queries, "within", split_axis=2, concat_axis=1, tiled=True),
        lax.all_to_all(keys_in, "within", split_axis=2, concat_axis=1, tiled=True),
        lax.all_to_all(values_in, "within", split_axis=2, concat_axis=1, tiled=True),
        lax.all_to_all(grad_out, "within", split_axis=2, concat_axis=1, tiled=True),
    )
    seq = q_wide.shape[1]
    cols = q_wide.shape[2]
    heads_here = cols // DH
    scale = DH ** (-0.5)

    def split_heads(block):
        return block.reshape(seq, heads_here, DH)

    query3 = split_heads(q_wide[0])
    key3 = split_heads(k_wide[0])
    value3 = split_heads(v_wide[0])
    cotan3 = split_heads(d_wide[0])
    group = lax.axis_index("frame")
    listed = partners[group]
    positions = jnp.arange(seq, dtype=jnp.int32)
    everyone = jnp.ones((seq,), jnp.float32)
    groups = lax.axis_size("frame") * queries.shape[0]

    def patches(other):
        return (positions >= registers[other]).astype(jnp.float32)

    def logits(keys_here, visible):
        raw = (
            jnp.einsum("qhd,khd->hqk", query3, keys_here, preferred_element_type=jnp.float32)
            * scale
        )
        return jnp.where(visible[None, None, :] > 0, raw, -1e30)

    def stats(state, keys_here, values_here, visible, weight):
        old_top, old_total, old_dsum = state
        raw = logits(keys_here, visible)
        top = jnp.max(raw, axis=2)
        expo = jnp.exp(raw - top[:, :, None])
        dprod = jnp.einsum("qhd,khd->hqk", cotan3, values_here, preferred_element_type=jnp.float32)
        total = weight * jnp.sum(expo, axis=2)
        dsum = weight * jnp.sum(expo * dprod, axis=2)
        new_top = jnp.maximum(old_top, top)
        keep_old = jnp.exp(old_top - new_top)
        keep_new = jnp.exp(top - new_top)
        return (
            new_top,
            old_total * keep_old + total * keep_new,
            old_dsum * keep_old + dsum * keep_new,
        )

    def grads(final, keys_here, values_here, visible, weight):
        top, total, delta = final
        raw = logits(keys_here, visible)
        prob = jnp.exp(raw - top[:, :, None]) / total[:, :, None]
        dprod = jnp.einsum("qhd,khd->hqk", cotan3, values_here, preferred_element_type=jnp.float32)
        dscore = prob * (dprod - delta[:, :, None])
        dscore_low = dscore.astype(jnp.bfloat16)
        dq_add = jnp.einsum(
            "hqk,khd->qhd", dscore_low, keys_here, preferred_element_type=jnp.float32
        ) * (scale * weight)
        prob_low = prob.astype(jnp.bfloat16)
        dk_add = jnp.einsum(
            "hqk,qhd->khd", dscore_low, query3, preferred_element_type=jnp.float32
        ) * (scale * weight)
        dv_add = (
            jnp.einsum("hqk,qhd->khd", prob_low, cotan3, preferred_element_type=jnp.float32)
            * weight
        )
        return (dq_add.reshape(seq, cols), dk_add.reshape(seq, cols), dv_add.reshape(seq, cols))

    blank = jnp.zeros((heads_here, seq), jnp.float32)
    state = stats((blank - 1e30, blank, blank), key3, value3, everyone, 1.0)
    keys_all, values_all = (
        lax.all_gather(k_wide, "frame", axis=0, tiled=True),
        lax.all_gather(v_wide, "frame", axis=0, tiled=True),
    )
    for slot in range(listed.shape[0]):
        other = listed[slot]
        state = stats(
            state, split_heads(keys_all[other]), split_heads(values_all[other]), patches(other), 1.0
        )
    top, total, dsum = state
    final = (top, total, dsum / total)
    own_terms = grads(final, key3, value3, everyone, 1.0)
    empty = jnp.zeros((groups, seq, cols), jnp.float32)
    results = (own_terms[0], empty.at[group].add(own_terms[1]), empty.at[group].add(own_terms[2]))
    for slot in range(listed.shape[0]):
        other = listed[slot]
        added = grads(
            final, split_heads(keys_all[other]), split_heads(values_all[other]), patches(other), 1.0
        )
        results = (
            results[0] + added[0],
            results[1].at[other].add(added[1]),
            results[2].at[other].add(added[2]),
        )
    dq_sum = results[0]
    dk_mine, dv_mine = (
        lax.psum_scatter(results[1], "frame", scatter_dimension=0, tiled=True),
        lax.psum_scatter(results[2], "frame", scatter_dimension=0, tiled=True),
    )
    dq_low = dq_sum.astype(jnp.bfloat16)[None]
    dk_low = dk_mine.astype(jnp.bfloat16)
    dv_low = dv_mine.astype(jnp.bfloat16)
    return (
        lax.all_to_all(dq_low, "within", split_axis=1, concat_axis=2, tiled=True),
        lax.all_to_all(dk_low, "within", split_axis=1, concat_axis=2, tiled=True),
        lax.all_to_all(dv_low, "within", split_axis=1, concat_axis=2, tiled=True),
    )


def solution(mesh):
    placed = (
        P("frame", "within", None),
        P("frame", "within", None),
        P("frame", "within", None),
        P("frame", "within", None),
        P(),
        P(),
    )
    return jax.shard_map(
        local,
        mesh=mesh,
        in_specs=placed,
        out_specs=(
            P("frame", "within", None),
            P("frame", "within", None),
            P("frame", "within", None),
        ),
        check_vma=False,
    )
```

profile of v0, /device:TPU:2, one launch (start us, length us, event | category | flops | bytes accessed | tf_op | source)
XLA Modules:
  0.0 439.2 jit_solution(8207483100817958708)
XLA Ops:
  7.2 1.3 copy.62
  9.0 2.3 reduce.55
  11.8 17.1 %all_to_all.120 = bf16[16,2,2304]{2,1,0:T(2,128)(2,1)S(1)} all-to-all(bf16[16,2,2304]{2,1,0:T(2,128)(2,1)S(1)} %reshape.625), channel_id=1, replica_groups=mesh['frame'=16,'within'=16] {'within'}, dimensions={0} | all-to-all | bytes 294912 | tf_op jit(solution)/shard_map/all_to_all | solution.py:12
  30.8 0.9 all_to_all.93
  31.8 1.2 copy.71
  33.1 2.3 reduce.57
  35.9 11.4 %all_to_all.121 = bf16[16,2,2304]{2,1,0:T(2,128)(2,1)S(1)} all-to-all(bf16[16,2,2304]{2,1,0:T(2,128)(2,1)S(1)} %reshape.621), channel_id=1, replica_groups=mesh['frame'=16,'within'=16] {'within'}, dimensions={0} | all-to-all | bytes 294912 | tf_op jit(solution)/shard_map/all_to_all | solution.py:13
  47.3 0.9 reshape.622
  49.2 0.9 all_to_all.100
  50.6 2.3 reduce.54
  52.9 1.2 reshape.623
  54.1 14.1 %all-to-all-start = ((bf16[16,2,2304]{2,1,0:T(2,128)(2,1)}), bf16[16,2,2304]{2,1,0:T(2,128)(2,1)S(1)}, u32[]{:S(2)}, u32[]{:S(2)}) async-start(bf16[16,2,2304]{2,1,0:T(2,128)(2,1)} %reshape.623), calls=%async_computation | async-start | bytes 294912 | tf_op jit(solution)/shard_map/all_to_all | solution.py:11
  71.4 2.3 reduce.56
  73.7 1.2 reshape.619
  76.6 9.3 %all-to-all-done = bf16[16,2,2304]{2,1,0:T(2,128)(2,1)S(1)} async-done(((bf16[16,2,2304]{2,1,0:T(2,128)(2,1)}), bf16[16,2,2304]{2,1,0:T(2,128)(2,1)S(1)}, u32[]{:S(2)}, u32[]{:S(2)}) %all-to-all-start) | async-done | bytes 147488 | tf_op jit(solution)/shard_map/all_to_all | solution.py:11
  86.0 3.5 all-to-all-start.2
  92.1 0.9 reshape.624
  94.3 3.6 all-to-all-done.2
  100.0 0.9 fusion.89
  101.0 2.4 copy-done.2
  103.4 3.6 fusion.2
  106.9 4.2 fusion.88
  111.2 4.2 fusion.87
  115.4 45.3 %all-gather.5.cloned.1.call-done = bf16[16,1152,64]{1,2,0:T(8,128)(2,1)} async-done(((bf16[1,1152,64]{1,2,0:T(8,128)(2,1)}), bf16[16,1152,64]{1,2,0:T(8,128)(2,1)}) %all-gather.5.cloned.1.call-update) | async-done | bytes 2359312 | tf_op jit(solution)/shard_map/all_gather | solution.py:85
  160.6 6.9 %fusion.3 = (f32[1152]{0:T(1024)S(1)}, f32[1152]{0:T(1024)S(1)}, f32[1152,1152]{0,1:T(8,128)}) fusion(f32[1152,1152]{0,1:T(8,128)} %get-tuple-element.98, f32[1152]{0:T(1024)S(1)} %get-tuple-element.97, bf16[1152,64]{0,1:T(8,128)(2,1)S(1)} %reshape.607, bf16[16,1152,64]{1,2,0:T(8,128)(2,1)} %all-gather.5.cloned.1.call-done, s32[]{:T(128)} %select_n.48), kind=kOutput, calls=%fused_computation.18 | convolution fusion | flops 175175424 | bytes 10926080 | tf_op jit(solution)/shard_map/qhd,khd->hqk/dot_general | solution.py:49
  167.5 5.6 %fusion.4 = (f32[1152]{0:T(1024)S(1)}, f32[1152]{0:T(1024)S(1)}, f32[1152,1152]{0,1:T(8,128)}) fusion(f32[1152,1152]{0,1:T(8,128)S(1)} %copy-done.3, f32[1152]{0:T(1024)S(1)} %get-tuple-element.94, bf16[1152,64]{0,1:T(8,128)(2,1)S(1)} %reshape.607, bf16[16,1152,64]{1,2,0:T(8,128)(2,1)} %all-gather.5.cloned.1.call-done, s32[]{:T(128)} %select_n.50), kind=kOutput, calls=%fused_computation.19 | convolution fusion | flops 175175424 | bytes 10926080 | tf_op jit(solution)/shard_map/qhd,khd->hqk/dot_general | solution.py:49
  173.2 8.1 %multiply_convert_fusion.1 = (bf16[1152,1152]{0,1:T(8,128)(2,1)S(1)}, bf16[1152,1152]{0,1:T(8,128)(2,1)S(1)}, bf16[1152,1152]{0,1:T(8,128)(2,1)S(1)}) fusion(f32[1152,1152]{0,1:T(8,128)} %get-tuple-element.101, f32[1152]{0:T(1024)S(1)} %get-tuple-element.84, f32[1152]{0:T(1024)S(1)} %get-tuple-element.83, f32[1152,1152]{0,1:T(8,128)S(1)} %bitcast.198, ...), kind=kLoop, calls=%fused_computation.6 | loop fusion | flops 19906560 | bytes 39826944 | tf_op jit(solution)/shard_map/convert_element_type | solution.py:67
  181.3 3.0 broadcast_in_dim.64.clone
  184.3 2.3 fusion.48
  186.7 2.8 fusion.53
  189.5 2.9 fusion.57
  192.5 2.9 broadcast_in_dim.64.clone.1
  195.4 6.3 %fusion.20 = f32[16,1152,64]{1,2,0:T(8,128)} fusion(f32[16,1152,64]{1,2,0:T(8,128)} %broadcast_in_dim.64.clone.1, s32[]{:T(128)} %select_n.47, bf16[1152,64]{0,1:T(8,128)(2,1)S(1)} %reshape.607, f32[1152,1152]{0,1:T(8,128)} %copy-done.2, f32[1152]{0:T(1024)S(1)} %get-tuple-element.83, f32[1152]{0:T(1024)S(1)} %get-tuple-element.88, pred[]{:T(512)} %get-tuple-element.91), kind=kOutput, calls=%fused_computation.37 | convolution fusion | flops 173924352 | bytes 5761024 | tf_op jit(solution)/shard_map/hqk,qhd->khd/dot_general | solution.py:76
  201.7 3.5 fusion.32
  205.3 3.6 fusion.44
  208.9 3.1 convolution_multiply_fusion.7
  212.6 1.9 fusion.59
  215.2 6.7 %reduce.58 = bf16[1152,64]{1,0:T(8,128)(2,1)S(1)} reduce(bf16[1152,1,64]{2,1,0:T(2,128)(2,1)S(1)} %bitcast.202, bf16[]{:T(256)} %broadcast.338), dimensions={1}, to_apply=%bitcast.158.reduce_sub_computation | reduce | bytes 294914
  222.7 4.8 %all-to-all-start.4 = ((bf16[16,2,2304]{2,1,0:T(2,128)(2,1)}), bf16[16,2,2304]{2,1,0:T(2,128)(2,1)S(1)}, u32[]{:S(2)}, u32[]{:S(2)}) async-start(bf16[16,2,2304]{2,1,0:T(2,128)(2,1)} %reshape.627), calls=%async_computation.4 | async-start | bytes 294912 | tf_op jit(solution)/shard_map/all_to_all | solution.py:116
  227.5 70.9 %reduce-scatter.3.cloned.1.call-done = f32[1,1152,64]{1,2,0:T(8,128)} async-done(((f32[16,1152,64]{1,2,0:T(8,128)}), f32[1,1152,64]{1,2,0:T(8,128)}) %reduce-scatter.3.cloned.1.call-update) | async-done | bytes 294928 | tf_op jit(solution)/shard_map/reduce_scatter | solution.py:109
  298.4 1.0 convert_element_type.67
  300.1 6.7 %reduce.59 = bf16[1152,64]{1,0:T(8,128)(2,1)S(1)} reduce(bf16[1152,1,64]{2,1,0:T(2,128)(2,1)S(1)} %bitcast.203, bf16[]{:T(256)} %broadcast.338), dimensions={1}, to_apply=%bitcast.160.reduce_sub_computation | reduce | bytes 294914
  307.7 4.5 %all-to-all-start.5 = ((bf16[16,2,2304]{2,1,0:T(2,128)(2,1)}), bf16[16,2,2304]{2,1,0:T(2,128)(2,1)S(1)}, u32[]{:S(2)}, u32[]{:S(2)}) async-start(bf16[16,2,2304]{2,1,0:T(2,128)(2,1)} %reshape.629), calls=%async_computation.6 | async-start | bytes 294912 | tf_op jit(solution)/shard_map/all_to_all | solution.py:117
  312.2 95.0 %reduce-scatter.5.cloned.1.call-done = f32[1,1152,64]{1,2,0:T(8,128)} async-done(((f32[16,1152,64]{1,2,0:T(8,128)}), f32[1,1152,64]{1,2,0:T(8,128)}) %reduce-scatter.5.cloned.1.call-update) | async-done | bytes 294928 | tf_op jit(solution)/shard_map/reduce_scatter | solution.py:110
  407.2 1.0 convert_element_type.71
  408.9 6.7 %reduce.60 = bf16[1152,64]{1,0:T(8,128)(2,1)S(1)} reduce(bf16[1152,1,64]{2,1,0:T(2,128)(2,1)S(1)} %bitcast.201, bf16[]{:T(256)} %broadcast.338), dimensions={1}, to_apply=%bitcast.162.reduce_sub_computation | reduce | bytes 294914
  416.5 4.6 %all-to-all-start.6 = ((bf16[16,2,2304]{2,1,0:T(2,128)(2,1)}), bf16[16,2,2304]{2,1,0:T(2,128)(2,1)S(1)}, u32[]{:S(2)}, u32[]{:S(2)}) async-start(bf16[16,2,2304]{2,1,0:T(2,128)(2,1)} %reshape.631), calls=%async_computation.8 | async-start | bytes 294912 | tf_op jit(solution)/shard_map/all_to_all | solution.py:118
  426.4 3.1 all-to-all-done.6
  (104 shorter events, 25.8 us)
Async XLA Ops:
  7.2 61.0 %copy-start = (s32[16,2]{0,1:T(2,128)S(1)}, s32[16,2]{0,1:T(2,128)}, u32[]{:S(2)}) copy-start(s32[16,2]{0,1:T(2,128)} %param.22) | copy-start | bytes 388
  7.2 43.0 %copy-start.7 = (bf16[1,72,1024]{2,1,0:T(8,128)(2,1)S(1)}, bf16[1,72,1024]{2,1,0:T(8,128)(2,1)}, u32[]{:S(2)}) copy-start(bf16[1,72,1024]{2,1,0:T(8,128)(2,1)} %param.18) | copy-start | bytes 442372
  7.2 99.7 %all-gather.3.cloned.1.call-start = ((), (), s32[]{:S(2)}) async-start(), calls=%async_computation.9 | async-start | bytes 2506752 | tf_op jit(solution)/shard_map/all_gather | solution.py:84
  11.8 59.2 %copy-start.8 = (bf16[1,72,1024]{2,1,0:T(8,128)(2,1)S(1)}, bf16[1,72,1024]{2,1,0:T(8,128)(2,1)}, u32[]{:S(2)}) copy-start(bf16[1,72,1024]{2,1,0:T(8,128)(2,1)} %param.21) | copy-start | bytes 442372
  30.2 45.8 %copy-start.9 = (s32[16]{0:T(128)S(1)}, s32[16]{0:T(128)}, u32[]{:S(2)}) copy-start(s32[16]{0:T(128)} %param.23) | copy-start | bytes 196
  30.4 60.3 %copy-start.10 = (s32[3]{0:T(128)S(1)}, s32[3]{0:T(128)}, u32[]{:S(2)}) copy-start(s32[3]{0:T(128)} %constant.142.clone.1) | copy-start | bytes 40
  31.8 128.8 %all-gather.5.cloned.1.call-start = ((), (), s32[]{:S(2)}) async-start(), calls=%async_computation.10 | async-start | bytes 2506752 | tf_op jit(solution)/shard_map/all_gather | solution.py:85
  54.1 31.9 %all-to-all-start = ((bf16[16,2,2304]{2,1,0:T(2,128)(2,1)}), bf16[16,2,2304]{2,1,0:T(2,128)(2,1)S(1)}, u32[]{:S(2)}, u32[]{:S(2)}) async-start(bf16[16,2,2304]{2,1,0:T(2,128)(2,1)} %reshape.623), calls=%async_computation | async-start | bytes 294912 | tf_op jit(solution)/shard_map/all_to_all | solution.py:11
  86.0 11.9 %all-to-all-start.2 = ((bf16[16,2,2304]{2,1,0:T(2,128)(2,1)}), bf16[16,2,2304]{2,1,0:T(2,128)(2,1)S(1)}, u32[]{:S(2)}, u32[]{:S(2)}) async-start(bf16[16,2,2304]{2,1,0:T(2,128)(2,1)} %reshape.619), calls=%async_computation.2 | async-start | bytes 294912 | tf_op jit(solution)/shard_map/all_to_all | solution.py:14
  89.5 208.9 %reduce-scatter.3.cloned.1.call-start = ((), (), s32[]{:S(2)}) async-start(), calls=%async_computation.11 | async-start | bytes 5013504 | tf_op jit(solution)/shard_map/reduce_scatter | solution.py:109
  101.0 2.4 copy-start.2
  160.6 6.9 %copy-start.3 = (f32[1152,1152]{0,1:T(8,128)S(1)}, f32[1152,1152]{0,1:T(8,128)}, u32[]{:S(2)}) copy-start(f32[1152,1152]{0,1:T(8,128)} %get-tuple-element.95) | copy-start | bytes 15925252
  160.6 12.6 %slice-start = ((s8[5308416]{0:T(1024)(128)(4,1)}), s8[4194304]{0:T(1024)(128)(4,1)S(1)}, s32[]{:S(2)}) async-start(s8[5308416]{0:T(1024)(128)(4,1)} %bitcast.193), calls=%async_computation.13 | async-start | bytes 8388608
  160.6 12.6 %slice-start.4 = ((s8[5308416]{0:T(1024)(128)(4,1)}), s8[4194304]{0:T(1024)(128)(4,1)S(1)}, s32[]{:S(2)}) async-start(s8[5308416]{0:T(1024)(128)(4,1)} %bitcast.197), calls=%async_computation.17 | async-start | bytes 8388608
  167.5 5.7 %slice-start.1 = ((s8[5308416]{0:T(1024)(128)(4,1)}), s8[1114112]{0:T(1024)(128)(4,1)S(1)}, s32[]{:S(2)}) async-start(s8[5308416]{0:T(1024)(128)(4,1)} %bitcast.193), calls=%async_computation.14 | async-start | bytes 2228224
  167.5 5.7 %slice-start.5 = ((s8[5308416]{0:T(1024)(128)(4,1)}), s8[1114112]{0:T(1024)(128)(4,1)S(1)}, s32[]{:S(2)}) async-start(s8[5308416]{0:T(1024)(128)(4,1)} %bitcast.197), calls=%async_computation.18 | async-start | bytes 2228224
  181.3 8.2 %copy-start.5 = (bf16[1152,1152]{0,1:T(8,128)(2,1)}, bf16[1152,1152]{0,1:T(8,128)(2,1)S(1)}, u32[]{:S(2)}) copy-start(bf16[1152,1152]{0,1:T(8,128)(2,1)S(1)} %get-tuple-element.85) | copy-start | bytes 7962628
  181.3 8.2 %copy-start.4 = (bf16[1152,1152]{0,1:T(8,128)(2,1)}, bf16[1152,1152]{0,1:T(8,128)(2,1)S(1)}, u32[]{:S(2)}) copy-start(bf16[1152,1152]{0,1:T(8,128)(2,1)S(1)} %get-tuple-element.86) | copy-start | bytes 7962628
  192.4 214.8 %reduce-scatter.5.cloned.1.call-start = ((), (), s32[]{:S(2)}) async-start(), calls=%async_computation.12 | async-start | bytes 5013504 | tf_op jit(solution)/shard_map/reduce_scatter | solution.py:110
  192.5 9.3 %slice-start.6 = ((s8[5308416]{0:T(1024)(128)(4,1)}), s8[4194304]{0:T(1024)(128)(4,1)S(1)}, s32[]{:S(2)}) async-start(s8[5308416]{0:T(1024)(128)(4,1)} %bitcast.199), calls=%async_computation.19 | async-start | bytes 8388608
  192.5 12.8 %slice-start.2 = ((s8[5308416]{0:T(1024)(128)(4,1)}), s8[4194304]{0:T(1024)(128)(4,1)S(1)}, s32[]{:S(2)}) async-start(s8[5308416]{0:T(1024)(128)(4,1)} %bitcast.195), calls=%async_computation.15 | async-start | bytes 8388608
  195.4 6.3 %slice-start.7 = ((s8[5308416]{0:T(1024)(128)(4,1)}), s8[1114112]{0:T(1024)(128)(4,1)S(1)}, s32[]{:S(2)}) async-start(s8[5308416]{0:T(1024)(128)(4,1)} %bitcast.199), calls=%async_computation.20 | async-start | bytes 2228224
  195.4 9.9 %slice-start.3 = ((s8[5308416]{0:T(1024)(128)(4,1)}), s8[1114112]{0:T(1024)(128)(4,1)S(1)}, s32[]{:S(2)}) async-start(s8[5308416]{0:T(1024)(128)(4,1)} %bitcast.195), calls=%async_computation.16 | async-start | bytes 2228224
  208.9 3.7 copy-start.6
  222.7 84.9 %all-to-all-start.4 = ((bf16[16,2,2304]{2,1,0:T(2,128)(2,1)}), bf16[16,2,2304]{2,1,0:T(2,128)(2,1)S(1)}, u32[]{:S(2)}, u32[]{:S(2)}) async-start(bf16[16,2,2304]{2,1,0:T(2,128)(2,1)} %reshape.627), calls=%async_computation.4 | async-start | bytes 294912 | tf_op jit(solution)/shard_map/all_to_all | solution.py:116
  307.7 108.8 %all-to-all-start.5 = ((bf16[16,2,2304]{2,1,0:T(2,128)(2,1)}), bf16[16,2,2304]{2,1,0:T(2,128)(2,1)S(1)}, u32[]{:S(2)}, u32[]{:S(2)}) async-start(bf16[16,2,2304]{2,1,0:T(2,128)(2,1)} %reshape.629), calls=%async_computation.6 | async-start | bytes 294912 | tf_op jit(solution)/shard_map/all_to_all | solution.py:117
  408.2 24.0 %copy-start.1 = (s32[16,2]{0,1:T(2,128)S(1)}, s32[16,2]{0,1:T(2,128)}, u32[]{:S(2)}) copy-start(s32[16,2]{0,1:T(2,128)} %param.22) | copy-start | bytes 388
  416.5 13.1 %all-to-all-start.6 = ((bf16[16,2,2304]{2,1,0:T(2,128)(2,1)}), bf16[16,2,2304]{2,1,0:T(2,128)(2,1)S(1)}, u32[]{:S(2)}, u32[]{:S(2)}) async-start(bf16[16,2,2304]{2,1,0:T(2,128)(2,1)} %reshape.631), calls=%async_computation.8 | async-start | bytes 294912 | tf_op jit(solution)/shard_map/all_to_all | solution.py:118
Sparse Core Ops, SparseCore 0:
  31.9 59.9 all-gather.2
  94.7 65.9 all-gather.4
  192.6 105.8 reduce-scatter.2
  303.2 103.9 reduce-scatter.4
where the time goes:
time: 448 us; the launch traced here: 439 us
  waiting for transfers between devices  227 us (51%)
  matrix products  52.5 us (12%)
  other arithmetic  41.3 us (9%)
  local copies, waits for them, and re-layouts  39.8 us (9%)
  starting transfers between devices  31.7 us (7%)
  blocking collectives  28.5 us (6%)
  between operations  18.1 us (4%)
    reduce_scatter x1, waiting for transfers between devices, local(): lax.psum_scatter(results[2], 'frame', scatter_dimension=0, tiled=True)  95 us
    reduce_scatter x1, waiting for transfers between devices, local(): lax.psum_scatter(results[1], 'frame', scatter_dimension=0, tiled=True)  70.9 us
    all_gather x1, waiting for transfers between devices, local(): lax.all_gather(v_wide, 'frame', axis=0, tiled=True)  45.3 us
    unnamed x11, other arithmetic  29.2 us
    all_to_all x1, blocking collectives, local(): lax.all_to_all(keys_in, 'within', split_axis=2, concat_axis=1, tiled=True)  17.1 us
    unnamed x57, local copies, waits for them, and re-layouts  16.9 us
    all_to_all x1, starting transfers between devices, local(): lax.all_to_all(queries, 'within', split_axis=2, concat_axis=1, tiled=True)  14.1 us
    dot_general x3, matrix products, grads(): jnp.einsum('hqk,qhd->khd', prob_low, cotan3, preferred_element_type=jnp.f...  13.4 us
  transfers between devices with their start and end apart: 9, of which 6 were waited for; matrix products, arithmetic and copies ran while one was open for 19% of the time, Pallas kernels for 0%

commit v1 on v0

--- a/solution.py
+++ b/solution.py
@@ -115,7 +115,12 @@
     return (
         lax.all_to_all(dq_low, "within", split_axis=1, concat_axis=2, tiled=True),
         lax.all_to_all(dk_low, "within", split_axis=1, concat_axis=2, tiled=True),
-        lax.all_to_all(dv_low, "within", split_axis=1, concat_axis=2, tiled=True),
+        jnp.concatenate(
+            lax.all_to_all(
+                jnp.stack(jnp.split(dv_low, lax.axis_size("within"), axis=1)), "within", 0, 0
+            ),
+            axis=2,
+        ),
     )
 
 

time: 448 us -> 453 us (1.011)
  local copies, waits for them, and re-layouts: 39.8 us -> 47.2 us
    reduce_scatter x1, waiting for transfers between devices: 95 us -> 64.9 us  [local(): lax.psum_scatter(results[2], 'frame', scatter_dimension=0, tiled=True)]
    reduce_scatter x1, waiting for transfers between devices: 70.9 us -> 99.2 us  [local(): lax.psum_scatter(results[1], 'frame', scatter_dimension=0, tiled=True)]
    unnamed x57 -> x63, local copies, waits for them, and re-layouts: 16.9 us -> 26.5 us
    all_to_all x1, waiting for transfers between devices: 0.01 us -> 7.11 us  [local(): lax.all_to_all(dk_low, 'within', split_axis=1, concat_axis=2, tiled=True)]
    unnamed x11 -> x8, other arithmetic: 29.2 us -> 23.4 us
  transfers between devices with their start and end apart: 9 -> 9, of which waited for: 6 -> 7; matrix products, arithmetic and copies ran while one was open for 19% -> 22% of each run, Pallas kernels for 0% -> 0%
where the time goes in v1:
time: 453 us; the launch traced here: 444 us
  waiting for transfers between devices  231 us (51%)
  matrix products  48.1 us (11%)
  local copies, waits for them, and re-layouts  47.2 us (10%)
  other arithmetic  40.1 us (9%)
  starting transfers between devices  31.6 us (7%)
  blocking collectives  28.5 us (6%)
  between operations  18.3 us (4%)
    reduce_scatter x1, waiting for transfers between devices, local(): lax.psum_scatter(results[1], 'frame', scatter_dimension=0, tiled=True)  99.2 us
    reduce_scatter x1, waiting for transfers between devices, local(): lax.psum_scatter(results[2], 'frame', scatter_dimension=0, tiled=True)  64.9 us
    all_gather x1, waiting for transfers between devices, local(): lax.all_gather(v_wide, 'frame', axis=0, tiled=True)  44.4 us
    unnamed x63, local copies, waits for them, and re-layouts  26.5 us
    unnamed x8, other arithmetic  23.4 us
    all_to_all x1, blocking collectives, local(): lax.all_to_all(keys_in, 'within', split_axis=2, concat_axis=1, tiled=True)  17.1 us
    all_to_all x1, starting transfers between devices, local(): lax.all_to_all(queries, 'within', split_axis=2, concat_axis=1, tiled=True)  15.2 us
    convert_element_type x1, other arithmetic, grads(): dscore_low = dscore.astype(jnp.bfloat16)  12.5 us
  transfers between devices with their start and end apart: 9, of which 7 were waited for; matrix products, arithmetic and copies ran while one was open for 22% of the time, Pallas kernels for 0%

profile of v1, /device:TPU:2, one launch (start us, length us, event | category | flops | bytes accessed | tf_op | source)
XLA Modules:
  0.0 444.4 jit_solution(3157966395684400098)
XLA Ops:
  7.2 1.3 copy.61
  9.1 2.4 reduce.55
  12.1 17.1 %all_to_all.107 = bf16[16,2,2304]{2,1,0:T(2,128)(2,1)S(1)} all-to-all(bf16[16,2,2304]{2,1,0:T(2,128)(2,1)S(1)} %reshape.633), channel_id=1, replica_groups=mesh['frame'=16,'within'=16] {'within'}, dimensions={0} | all-to-all | bytes 294912 | tf_op jit(solution)/shard_map/all_to_all | solution.py:12
  31.1 0.9 all_to_all.83
  32.1 1.2 copy.70
  33.4 2.4 reduce.57
  36.3 11.4 %all_to_all.108 = bf16[16,2,2304]{2,1,0:T(2,128)(2,1)S(1)} all-to-all(bf16[16,2,2304]{2,1,0:T(2,128)(2,1)S(1)} %reshape.629), channel_id=1, replica_groups=mesh['frame'=16,'within'=16] {'within'}, dimensions={0} | all-to-all | bytes 294912 | tf_op jit(solution)/shard_map/all_to_all | solution.py:13
  47.7 0.9 reshape.630
  49.6 0.9 all_to_all.90
  51.0 2.4 reduce.54
  53.4 1.2 reshape.631
  54.6 15.2 %all-to-all-start = ((bf16[16,2,2304]{2,1,0:T(2,128)(2,1)}), bf16[16,2,2304]{2,1,0:T(2,128)(2,1)S(1)}, u32[]{:S(2)}, u32[]{:S(2)}) async-start(bf16[16,2,2304]{2,1,0:T(2,128)(2,1)} %reshape.631), calls=%async_computation | async-start | bytes 294912 | tf_op jit(solution)/shard_map/all_to_all | solution.py:11
  73.3 2.4 reduce.56
  75.7 1.2 reshape.627
  78.8 8.2 %all-to-all-done = bf16[16,2,2304]{2,1,0:T(2,128)(2,1)S(1)} async-done(((bf16[16,2,2304]{2,1,0:T(2,128)(2,1)}), bf16[16,2,2304]{2,1,0:T(2,128)(2,1)S(1)}, u32[]{:S(2)}, u32[]{:S(2)}) %all-to-all-start) | async-done | bytes 147488 | tf_op jit(solution)/shard_map/all_to_all | solution.py:11
  87.0 3.5 all-to-all-start.2
  93.3 0.9 reshape.632
  95.4 3.4 all-to-all-done.2
  101.0 0.9 fusion.89
  102.0 2.3 copy-done.2
  104.2 3.7 fusion.2
  107.9 4.2 fusion.88
  112.1 4.2 fusion.87
  116.4 44.4 %all-gather.5.cloned.1.call-done = bf16[16,1152,64]{1,2,0:T(8,128)(2,1)} async-done(((bf16[1,1152,64]{1,2,0:T(8,128)(2,1)}), bf16[16,1152,64]{1,2,0:T(8,128)(2,1)}) %all-gather.5.cloned.1.call-update) | async-done | bytes 2359312 | tf_op jit(solution)/shard_map/all_gather | solution.py:85
  160.7 6.6 %fusion.3 = (f32[1152]{0:T(1024)S(1)}, f32[1152]{0:T(1024)S(1)}, f32[1152,1152]{0,1:T(8,128)}) fusion(f32[1152,1152]{0,1:T(8,128)} %get-tuple-element.110, f32[1152]{0:T(1024)S(1)} %get-tuple-element.109, bf16[1152,64]{0,1:T(8,128)(2,1)S(1)} %reshape.613, bf16[16,1152,64]{1,2,0:T(8,128)(2,1)} %all-gather.5.cloned.1.call-done, s32[]{:T(128)} %select_n.48), kind=kOutput, calls=%fused_computation.18 | convolution fusion | flops 175175424 | bytes 10926080 | tf_op jit(solution)/shard_map/qhd,khd->hqk/dot_general | solution.py:49
  167.3 5.1 %fusion.4 = (f32[1152]{0:T(1024)S(1)}, f32[1152]{0:T(1024)S(1)}, f32[1152,1152]{0,1:T(8,128)}) fusion(f32[1152,1152]{0,1:T(8,128)S(1)} %copy-done.3, f32[1152]{0:T(1024)S(1)} %get-tuple-element.106, bf16[1152,64]{0,1:T(8,128)(2,1)S(1)} %reshape.613, bf16[16,1152,64]{1,2,0:T(8,128)(2,1)} %all-gather.5.cloned.1.call-done, s32[]{:T(128)} %select_n.50), kind=kOutput, calls=%fused_computation.19 | convolution fusion | flops 175175424 | bytes 10926080 | tf_op jit(solution)/shard_map/qhd,khd->hqk/dot_general | solution.py:49
  172.4 2.9 broadcast_in_dim.64.clone.1
  175.3 2.6 fusion.20
  177.9 3.6 fusion.32
  181.6 3.6 fusion.44
  185.2 12.5 %multiply_convert_fusion.1 = (bf16[1152,1152]{0,1:T(8,128)(2,1)S(1)}, bf16[1152,1152]{0,1:T(8,128)(2,1)S(1)}, bf16[1152,1152]{0,1:T(8,128)(2,1)S(1)}) fusion(f32[1152,1152]{0,1:T(8,128)} %get-tuple-element.113, f32[1152]{0:T(1024)S(1)} %get-tuple-element.96, f32[1152]{0:T(1024)S(1)} %get-tuple-element.95, f32[1152,1152]{0,1:T(8,128)} %get-tuple-element.110, ...), kind=kLoop, calls=%fused_computation.6 | loop fusion | flops 19906560 | bytes 39826944 | tf_op jit(solution)/shard_map/convert_element_type | solution.py:67
  197.8 2.9 broadcast_in_dim.64.clone
  200.7 2.3 fusion.48
  203.0 3.0 fusion.53
  206.0 2.9 fusion.57
  209.0 2.9 convolution_multiply_fusion.7
  212.5 1.9 fusion.59
  215.1 6.8 %reduce.58 = bf16[1152,64]{1,0:T(8,128)(2,1)S(1)} reduce(bf16[1152,1,64]{2,1,0:T(2,128)(2,1)S(1)} %bitcast.258, bf16[]{:T(256)} %broadcast.338), dimensions={1}, to_apply=%bitcast.220.reduce_sub_computation | reduce | bytes 294914
  222.7 4.4 all-to-all-start.4
  227.2 64.9 %reduce-scatter.5.cloned.1.call-done = f32[1,1152,64]{1,2,0:T(8,128)} async-done(((f32[16,1152,64]{1,2,0:T(8,128)}), f32[1,1152,64]{1,2,0:T(8,128)}) %reduce-scatter.5.cloned.1.call-update) | async-done | bytes 294928 | tf_op jit(solution)/shard_map/reduce_scatter | solution.py:110
  292.0 1.0 convert_element_type.71
  301.7 99.2 %reduce-scatter.3.cloned.1.call-done = f32[1,1152,64]{1,2,0:T(8,128)} async-done(((f32[16,1152,64]{1,2,0:T(8,128)}), f32[1,1152,64]{1,2,0:T(8,128)}) %reduce-scatter.3.cloned.1.call-update) | async-done | bytes 294928 | tf_op jit(solution)/shard_map/reduce_scatter | solution.py:109
  400.9 1.0 convert_element_type.67
  402.6 6.8 %reduce.59 = bf16[1152,64]{1,0:T(8,128)(2,1)S(1)} reduce(bf16[1152,1,64]{2,1,0:T(2,128)(2,1)S(1)} %bitcast.257, bf16[]{:T(256)} %broadcast.338), dimensions={1}, to_apply=%bitcast.222.reduce_sub_computation | reduce | bytes 294914
  411.0 4.6 %all-to-all-start.5 = ((bf16[16,2,2304]{2,1,0:T(2,128)(2,1)}), bf16[16,2,2304]{2,1,0:T(2,128)(2,1)S(1)}, u32[]{:S(2)}, u32[]{:S(2)}) async-start(bf16[16,2,2304]{2,1,0:T(2,128)(2,1)} %reshape.637), calls=%async_computation.6 | async-start | bytes 294912 | tf_op jit(solution)/shard_map/all_to_all | solution.py:117
  416.9 7.1 %all-to-all-done.5 = bf16[16,2,2304]{2,1,0:T(2,128)(2,1)S(1)} async-done(((bf16[16,2,2304]{2,1,0:T(2,128)(2,1)}), bf16[16,2,2304]{2,1,0:T(2,128)(2,1)S(1)}, u32[]{:S(2)}, u32[]{:S(2)}) %all-to-all-start.5) | async-done | bytes 147488 | tf_op jit(solution)/shard_map/all_to_all | solution.py:117
  424.0 3.8 all-to-all-start.6
  433.2 3.5 all-to-all-done.6
  (103 shorter events, 33.5 us)
Async XLA Ops:
  7.2 62.6 %copy-start = (s32[16,2]{0,1:T(2,128)S(1)}, s32[16,2]{0,1:T(2,128)}, u32[]{:S(2)}) copy-start(s32[16,2]{0,1:T(2,128)} %param.22) | copy-start | bytes 388
  7.2 43.4 %copy-start.7 = (bf16[1,72,1024]{2,1,0:T(8,128)(2,1)S(1)}, bf16[1,72,1024]{2,1,0:T(8,128)(2,1)}, u32[]{:S(2)}) copy-start(bf16[1,72,1024]{2,1,0:T(8,128)(2,1)} %param.18) | copy-start | bytes 442372
  7.2 100.7 %all-gather.3.cloned.1.call-start = ((), (), s32[]{:S(2)}) async-start(), calls=%async_computation.9 | async-start | bytes 2506752 | tf_op jit(solution)/shard_map/all_gather | solution.py:84
  12.1 60.8 %copy-start.8 = (bf16[1,72,1024]{2,1,0:T(8,128)(2,1)S(1)}, bf16[1,72,1024]{2,1,0:T(8,128)(2,1)}, u32[]{:S(2)}) copy-start(bf16[1,72,1024]{2,1,0:T(8,128)(2,1)} %param.21) | copy-start | bytes 442372
  30.4 47.7 %copy-start.9 = (s32[16]{0:T(128)S(1)}, s32[16]{0:T(128)}, u32[]{:S(2)}) copy-start(s32[16]{0:T(128)} %param.23) | copy-start | bytes 196
  30.7 61.2 %copy-start.10 = (s32[3]{0:T(128)S(1)}, s32[3]{0:T(128)}, u32[]{:S(2)}) copy-start(s32[3]{0:T(128)} %constant.142.clone.1) | copy-start | bytes 40
  32.0 128.7 %all-gather.5.cloned.1.call-start = ((), (), s32[]{:S(2)}) async-start(), calls=%async_computation.10 | async-start | bytes 2506752 | tf_op jit(solution)/shard_map/all_gather | solution.py:85
  54.6 32.4 %all-to-all-start = ((bf16[16,2,2304]{2,1,0:T(2,128)(2,1)}), bf16[16,2,2304]{2,1,0:T(2,128)(2,1)S(1)}, u32[]{:S(2)}, u32[]{:S(2)}) async-start(bf16[16,2,2304]{2,1,0:T(2,128)(2,1)} %reshape.631), calls=%async_computation | async-start | bytes 294912 | tf_op jit(solution)/shard_map/all_to_all | solution.py:11
  87.0 11.9 %all-to-all-start.2 = ((bf16[16,2,2304]{2,1,0:T(2,128)(2,1)}), bf16[16,2,2304]{2,1,0:T(2,128)(2,1)S(1)}, u32[]{:S(2)}, u32[]{:S(2)}) async-start(bf16[16,2,2304]{2,1,0:T(2,128)(2,1)} %reshape.627), calls=%async_computation.2 | async-start | bytes 294912 | tf_op jit(solution)/shard_map/all_to_all | solution.py:14
  90.5 201.6 %reduce-scatter.5.cloned.1.call-start = ((), (), s32[]{:S(2)}) async-start(), calls=%async_computation.12 | async-start | bytes 5013504 | tf_op jit(solution)/shard_map/reduce_scatter | solution.py:110
  102.0 2.3 copy-start.2
  160.7 6.6 %copy-start.3 = (f32[1152,1152]{0,1:T(8,128)S(1)}, f32[1152,1152]{0,1:T(8,128)}, u32[]{:S(2)}) copy-start(f32[1152,1152]{0,1:T(8,128)} %get-tuple-element.107) | copy-start | bytes 15925252
  160.7 14.6 %slice-start = ((s8[5308416]{0:T(1024)(128)(4,1)}), s8[4194304]{0:T(1024)(128)(4,1)S(1)}, s32[]{:S(2)}) async-start(s8[5308416]{0:T(1024)(128)(4,1)} %bitcast.253), calls=%async_computation.13 | async-start | bytes 8388608
  167.3 8.0 %slice-start.1 = ((s8[5308416]{0:T(1024)(128)(4,1)}), s8[1114112]{0:T(1024)(128)(4,1)S(1)}, s32[]{:S(2)}) async-start(s8[5308416]{0:T(1024)(128)(4,1)} %bitcast.253), calls=%async_computation.14 | async-start | bytes 2228224
  172.4 5.5 %slice-start.2 = ((s8[5308416]{0:T(1024)(128)(4,1)}), s8[4194304]{0:T(1024)(128)(4,1)S(1)}, s32[]{:S(2)}) async-start(s8[5308416]{0:T(1024)(128)(4,1)} %bitcast.255), calls=%async_computation.15 | async-start | bytes 8388608
  175.3 2.6 slice-start.3
  185.2 215.8 %reduce-scatter.3.cloned.1.call-start = ((), (), s32[]{:S(2)}) async-start(), calls=%async_computation.11 | async-start | bytes 5013504 | tf_op jit(solution)/shard_map/reduce_scatter | solution.py:109
  197.7 8.3 %copy-start.5 = (bf16[1152,1152]{0,1:T(8,128)(2,1)}, bf16[1152,1152]{0,1:T(8,128)(2,1)S(1)}, u32[]{:S(2)}) copy-start(bf16[1152,1152]{0,1:T(8,128)(2,1)S(1)} %get-tuple-element.97) | copy-start | bytes 7962628
  197.8 8.3 %copy-start.4 = (bf16[1152,1152]{0,1:T(8,128)(2,1)}, bf16[1152,1152]{0,1:T(8,128)(2,1)S(1)}, u32[]{:S(2)}) copy-start(bf16[1152,1152]{0,1:T(8,128)(2,1)S(1)} %get-tuple-element.98) | copy-start | bytes 7962628
  209.0 3.5 copy-start.6
  222.7 188.2 %all-to-all-start.4 = ((bf16[16,2,2304]{2,1,0:T(2,128)(2,1)}), bf16[16,2,2304]{2,1,0:T(2,128)(2,1)S(1)}, u32[]{:S(2)}, u32[]{:S(2)}) async-start(bf16[16,2,2304]{2,1,0:T(2,128)(2,1)} %reshape.635), calls=%async_computation.4 | async-start | bytes 294912 | tf_op jit(solution)/shard_map/all_to_all | solution.py:116
  227.1 210.3 %copy-start.1 = (s32[16,2]{0,1:T(2,128)S(1)}, s32[16,2]{0,1:T(2,128)}, u32[]{:S(2)}) copy-start(s32[16,2]{0,1:T(2,128)} %param.22) | copy-start | bytes 388
  411.0 13.1 %all-to-all-start.5 = ((bf16[16,2,2304]{2,1,0:T(2,128)(2,1)}), bf16[16,2,2304]{2,1,0:T(2,128)(2,1)S(1)}, u32[]{:S(2)}, u32[]{:S(2)}) async-start(bf16[16,2,2304]{2,1,0:T(2,128)(2,1)} %reshape.637), calls=%async_computation.6 | async-start | bytes 294912 | tf_op jit(solution)/shard_map/all_to_all | solution.py:117
  424.0 12.6 %all-to-all-start.6 = ((bf16[16,1,72,64]{2,3,1,0:T(8,128)(2,1)}), bf16[16,1,72,64]{2,3,1,0:T(8,128)(2,1)S(1)}, u32[]{:S(2)}, u32[]{:S(2)}) async-start(bf16[16,1,72,64]{2,3,1,0:T(8,128)(2,1)} %constant_dynamic-update-slice_fusion), calls=%async_computation.8 | async-start | bytes 524288 | tf_op jit(solution)/shard_map/all_to_all | solution.py:119
Sparse Core Ops, SparseCore 0:
  32.2 61.7 all-gather.2
  96.7 63.9 all-gather.4
  185.3 106.7 reduce-scatter.4
  296.9 104.0 reduce-scatter.2
